TPU v7x, 512 devices: a whole 4x8x8 slice. The times are simulated.
512 devices in a mesh: row: 16 (over z, core), col: 32 (over y, x).
Axes of the slice: x: 4, y: 8, z: 8, core: 2. Of those that a mesh axis runs over, the one named last changes fastest.
Arguments:
- rhs: bfloat16 [57344, 256], P('row', 'col'), may hold values from -6 to 6
- dinv: bfloat16 [224, 256, 256], P('row'), may hold values from -1 to 2.5, as said below
- blocks: bfloat16 [16, 448, 256, 256], P('row', 'col'), may hold values from -0.046875 to 0.046875
- block_row: int32 [16, 448], P('row', 'col'), may hold values from 0 to 14, as said below
- block_col: int32 [16, 448], P('row', 'col'), may hold values from 0 to 223, as said below
Outputs:
- solution: bfloat16 [57344, 256], P('row', 'col')
Inputs may be any that keep to these rules, and one draw needn't show every extreme that they name: `dinv`: lower triangular with positive diagonal. `block_row`: slots at positions below 8 of a device hold level-1 row supernodes, the others level-2 ones; 14 marks an empty slot. Some device fills all its slots. `block_col`: A live slot's column supernode is congruent to the device's col index modulo 32 and has a lower level than its row supernode; no pair of supernodes is held twice. An empty slot holds the device's col index.
All inputs are finite; a program needn't handle non-finite values.
Results may differ from a plain program's by a relative error of at most 0.028.
Values may be sent and summed in bfloat16 or wider, within the bound.
No kernel may reach another device: no remote copies, remote signals or barrier semaphores. Data moves between devices by JAX's collectives and lax.ppermute only.
A program may use at most 64 MiB of HBM per device.

v0:
```python
import jax
import jax.numpy as jnp
from jax import lax
from jax.sharding import PartitionSpec as P

L0 = 8
L1 = 4
L2 = 2
SLOTS1 = 8


def solve_rows(factor, vector):
    return jnp.einsum(
        "kab,kbn->kan", factor, vector.astype(jnp.bfloat16), preferred_element_type=jnp.float32
    ).astype(jnp.bfloat16)


def solve_cols(factor, vector):
    return jnp.einsum(
        "kab,kan->kbn", factor, vector.astype(jnp.bfloat16), preferred_element_type=jnp.float32
    ).astype(jnp.bfloat16)


def pick_rows(table, index, valid):
    final_row = table.shape[0] - 1
    chosen = lax.dynamic_index_in_dim(table, jnp.clip(index, 0, final_row), 0, keepdims=False)
    return jnp.where(valid, chosen, jnp.zeros_like(chosen))


def forward_level(tiles, row_list, source, first, count, target_part, factor_part):
    product = jnp.einsum("sab,sbn->san", tiles, source, preferred_element_type=jnp.float32)
    onehot = (row_list[:, None] == first + jnp.arange(count, dtype=jnp.int32)[None, :]).astype(
        jnp.float32
    )
    partial_sum = jnp.einsum("sk,san->kan", onehot, product)
    summed = lax.psum(partial_sum.astype(jnp.bfloat16), "col").astype(jnp.float32)
    return solve_rows(factor_part, target_part - summed)


def send_panels(full, first_k, owned):
    pieces = [pick_rows(full, first_k + 0, first_k + 0 < owned)]
    return lax.all_gather(jnp.stack(pieces), "row", axis=0, tiled=True)


def carry_terms(tiles, row_list, known):
    padded = jnp.concatenate([known, jnp.zeros((1,) + known.shape[1:], jnp.bfloat16)])
    chosen = jnp.take(padded, row_list, axis=0)
    return jnp.einsum("sab,san->sbn", tiles, chosen, preferred_element_type=jnp.float32)


def scatter_carry(terms, col_list, owned, col_count, row_count, per_dev):
    slot_target = col_list // owned * per_dev + col_list % owned // col_count
    onehot = (
        slot_target[:, None] == jnp.arange(row_count * per_dev, dtype=jnp.int32)[None, :]
    ).astype(jnp.float32)
    return lax.psum_scatter(
        jnp.einsum("sq,sbn->qbn", onehot, terms).astype(jnp.bfloat16),
        "row",
        scatter_dimension=0,
        tiled=True,
    ).astype(jnp.float32)


def on_device(rhs, dinv, blocks, block_row, block_col):
    row_count = lax.axis_size("row")
    col_count = lax.axis_size("col")
    row_id = lax.axis_index("row")
    col_id = lax.axis_index("col")
    middle = L0 + L1
    owned = L0 + L1 + L2
    per_dev = -(-owned // col_count)
    whole = lax.all_gather(rhs, "col", axis=1, tiled=True)
    height = dinv.shape[1]
    breadth = whole.shape[1]
    part_width = breadth // col_count
    target = whole.reshape(owned, height, breadth).astype(jnp.float32)
    tiles_one = blocks[0, :SLOTS1]
    tiles_two = blocks[0, SLOTS1:]
    rows_one = block_row[0, :SLOTS1]
    rows_two = block_row[0, SLOTS1:]
    cols_one = block_col[0, :SLOTS1]
    cols_two = block_col[0, SLOTS1:]
    cols_all = block_col[0]
    first_k = (col_id - owned * row_id) % col_count
    source_one = cols_one // owned * per_dev + cols_one % owned // col_count
    source_two = cols_two // owned * per_dev + cols_two % owned // col_count
    zeros_low = jnp.zeros((L0, height, breadth), jnp.bfloat16)
    zeros_mid = jnp.zeros((L1, height, breadth), jnp.bfloat16)
    zeros_top = jnp.zeros((L2, height, breadth), jnp.bfloat16)
    y_low = solve_rows(dinv[:L0], target[:L0])
    panels_low = send_panels(jnp.concatenate([y_low, zeros_mid, zeros_top]), first_k, owned)
    y_mid = forward_level(
        tiles_one,
        rows_one,
        jnp.take(panels_low, source_one, axis=0),
        L0,
        L1,
        target[L0:middle],
        dinv[L0:middle],
    )
    panels_mid = send_panels(jnp.concatenate([zeros_low, y_mid, zeros_top]), first_k, owned)
    panels_all = panels_low + panels_mid
    y_top = forward_level(
        tiles_two,
        rows_two,
        jnp.take(panels_all, source_two, axis=0),
        middle,
        L2,
        target[middle:],
        dinv[middle:],
    )
    y_all = jnp.concatenate([y_low, y_mid, y_top])
    x_top = solve_cols(dinv[middle:], y_top)
    terms_two = carry_terms(tiles_two, rows_two, jnp.concatenate([zeros_low, zeros_mid, x_top]))
    local_ks = [first_k + 0]
    factors = [
        lax.dynamic_index_in_dim(dinv, jnp.minimum(local_k, owned - 1), 0, keepdims=True)
        for local_k in local_ks
    ]
    y_owned = [
        pick_rows(y_all, local_k, local_k < owned).astype(jnp.float32) for local_k in local_ks
    ]
    carry_first = scatter_carry(terms_two, cols_two, owned, col_count, row_count, per_dev)
    carry_top = [carry_first[0]]
    mid_slots = L0 + jnp.arange(L1, dtype=jnp.int32)
    member = 0
    x_owned = solve_cols(factors[member], (y_owned[member] - carry_top[member])[None])
    spread = jnp.where(
        (mid_slots == local_ks[member])[:, None, None], x_owned, jnp.zeros_like(x_owned)
    )
    x_mid = lax.psum(spread, "col").astype(jnp.float32).astype(jnp.bfloat16)
    terms_one = carry_terms(tiles_one, rows_one, jnp.concatenate([zeros_low, x_mid, x_top]))
    terms_all = jnp.concatenate([terms_one, terms_two])
    carry_second = scatter_carry(terms_all, cols_all, owned, col_count, row_count, per_dev)
    residues = [y_owned[0] - carry_second[0]]
    outgoing = []
    member = 0
    x_owned = solve_cols(factors[member], residues[member][None])[0]
    outgoing.append(jnp.where(local_ks[member] < L0, x_owned, jnp.zeros_like(x_owned)))
    outgoing = jnp.stack(outgoing).reshape(per_dev, height, col_count, part_width)
    outgoing = outgoing.transpose(2, 0, 1, 3).reshape(col_count, per_dev * height * part_width)
    incoming = lax.all_to_all(outgoing, "col", split_axis=0, concat_axis=0, tiled=True)
    low_ks = jnp.arange(L0, dtype=jnp.int32)
    sources = (row_id * owned + low_ks) % col_count * per_dev + low_ks // col_count
    x_low = jnp.take(incoming, sources, axis=0).reshape(L0, height, part_width)
    upper = lax.dynamic_slice_in_dim(
        jnp.concatenate([x_mid, x_top]), col_id * part_width, part_width, 2
    )
    return jnp.concatenate([x_low, upper]).reshape(owned * height, part_width)


def solution(mesh):
    placed = (
        P("row", "col"),
        P("row", None, None),
        P("row", "col", None, None),
        P("row", "col"),
        P("row", "col"),
    )
    return jax.shard_map(
        on_device, mesh=mesh, in_specs=placed, out_specs=P("row", "col"), check_vma=False
    )
```

profile of v0, /device:TPU:8, one launch (start us, length us, event | category | flops | bytes accessed | tf_op | source)
XLA Modules:
  0.0 870.5 jit_solution(18008842323864152416)
XLA Ops:
  6.5 0.7 all-gather.4.cloned.1.call-update
  7.3 0.6 pad_dynamic-slice_fusion.7
  7.9 88.9 %all-gather.4.cloned.1.call-done = bf16[3584,256]{0,1:T(8,128)(2,1)} async-done(((bf16[3584,8]{0,1:T(8,128)(2,1)}), bf16[3584,256]{0,1:T(8,128)(2,1)}) %all-gather.4.cloned.1.call-update) | async-done | bytes 1835024 | tf_op jit(solution)/shard_map/all_gather | solution.py:72
  96.8 2.3 slice.69
  99.1 1.5 copy.103
  100.6 0.4 convolution_convert_fusion
  101.2 1.0 copy-done.1
  102.1 0.8 copy-done.2
  102.9 1.4 maximum_select_fusion
  104.5 41.9 %all-gather.6.cloned.1.call-done = bf16[16,256,256]{2,1,0:T(8,128)(2,1)} async-done(((bf16[1,256,256]{2,1,0:T(8,128)(2,1)}), bf16[16,256,256]{2,1,0:T(8,128)(2,1)}) %all-gather.6.cloned.1.call-update) | async-done | bytes 2097168 | tf_op jit(solution)/shard_map/all_gather | solution.py:42
  146.4 2.2 gather_fusion
  148.6 2.8 convolution_bitcast_fusion.1
  151.4 1.9 copy.106
  153.3 0.5 fusion.58
  153.7 0.9 copy.145
  154.7 2.1 slice.70
  156.8 1.6 copy.150
  158.4 151.8 %all-reduce.4.cloned.1.call-done = bf16[4,256,256]{2,1,0:T(8,128)(2,1)} async-done(((bf16[4,256,256]{2,1,0:T(8,128)(2,1)}), bf16[4,256,256]{2,1,0:T(8,128)(2,1)}) %all-reduce.4.cloned.1.call-update) | async-done | bytes 524304 | tf_op jit(solution)/shard_map/psum | solution.py:36
  310.2 1.4 fusion
  311.7 1.4 maximum_select_fusion.1
  313.5 41.2 %all-gather.8.cloned.1.call-done = bf16[16,256,256]{2,1,0:T(8,128)(2,1)} async-done(((bf16[1,256,256]{2,1,0:T(8,128)(2,1)}), bf16[16,256,256]{2,1,0:T(8,128)(2,1)}) %all-gather.8.cloned.1.call-update) | async-done | bytes 2097168 | tf_op jit(solution)/shard_map/all_gather | solution.py:42
  354.7 4.2 add.346
  358.9 3.1 gather_fusion.1
  362.0 2.8 convolution_bitcast_fusion.3
  364.8 2.6 copy.111
  367.4 1.7 fusion.54
  369.1 0.7 copy.146
  369.9 0.6 compare_and_fusion
  370.5 1.8 slice.71
  372.3 2.0 copy.149
  374.3 148.0 %all-reduce.6.cloned.1.call-done = bf16[2,256,256]{2,1,0:T(8,128)(2,1)} async-done(((bf16[2,256,256]{2,1,0:T(8,128)(2,1)}), bf16[2,256,256]{2,1,0:T(8,128)(2,1)}) %all-reduce.6.cloned.1.call-update) | async-done | bytes 262160 | tf_op jit(solution)/shard_map/psum | solution.py:36
  522.3 1.4 convolution_convert_fusion.2
  523.7 0.7 copy-done.7
  524.4 0.3 fusion.1
  524.7 0.7 copy-done.4
  525.4 1.6 pad_maximum_fusion.2
  527.0 3.0 gather_fusion.2
  530.1 2.8 convolution_bitcast_fusion.2
  532.9 2.6 copy.118
  535.4 2.1 fusion.46
  537.5 2.0 copy.144
  539.7 1.7 broadcast_select_fusion.2
  541.3 59.4 %reduce-scatter.3.cloned.1.call-done = bf16[1,256,256]{2,1,0:T(8,128)(2,1)} async-done(((bf16[16,256,256]{2,1,0:T(8,128)(2,1)}), bf16[1,256,256]{2,1,0:T(8,128)(2,1)}) %reduce-scatter.3.cloned.1.call-update) | async-done | bytes 131088 | tf_op jit(solution)/shard_map/reduce_scatter | solution.py:56
  600.7 1.2 convolution_convert_fusion.5
  601.9 0.9 broadcast_select_fusion
  603.1 156.6 %all-reduce.8.cloned.1.call-done = bf16[4,256,256]{2,1,0:T(8,128)(2,1)} async-done(((bf16[4,256,256]{2,1,0:T(8,128)(2,1)}), bf16[4,256,256]{2,1,0:T(8,128)(2,1)}) %all-reduce.8.cloned.1.call-update) | async-done | bytes 524304 | tf_op jit(solution)/shard_map/psum | solution.py:131
  759.8 2.6 pad_maximum_fusion.1
  762.4 2.2 gather_fusion.3
  764.6 1.9 convolution_bitcast_fusion
  766.5 1.4 pad_maximum_fusion
  767.8 4.5 copy.121
  772.4 2.3 fusion.42
  774.6 2.0 copy.143
  776.7 61.1 %reduce-scatter.5.cloned.1.call-done = bf16[1,256,256]{2,1,0:T(8,128)(2,1)} async-done(((bf16[16,256,256]{2,1,0:T(8,128)(2,1)}), bf16[1,256,256]{2,1,0:T(8,128)(2,1)}) %reduce-scatter.5.cloned.1.call-update) | async-done | bytes 131088 | tf_op jit(solution)/shard_map/reduce_scatter | solution.py:56
  837.9 1.1 fusion.3
  839.0 0.3 copy.123
  839.4 0.5 broadcast.811
  839.9 1.1 reduce
  841.2 0.7 reshape.589
  841.9 9.8 %all-to-all-start = ((bf16[32,2,1024]{2,1,0:T(2,128)(2,1)}), bf16[32,2,1024]{2,1,0:T(2,128)(2,1)S(1)}, u32[]{:S(2)}, u32[]{:S(2)}) async-start(bf16[32,2,1024]{2,1,0:T(2,128)(2,1)} %reshape.589), calls=%async_computation.2 | async-start | bytes 262144 | tf_op jit(solution)/shard_map/all_to_all | solution.py:142
  852.2 9.2 %all-to-all-done = bf16[32,2,1024]{2,1,0:T(2,128)(2,1)S(1)} async-done(((bf16[32,2,1024]{2,1,0:T(2,128)(2,1)}), bf16[32,2,1024]{2,1,0:T(2,128)(2,1)S(1)}, u32[]{:S(2)}, u32[]{:S(2)}) %all-to-all-start) | async-done | bytes 131104 | tf_op jit(solution)/shard_map/all_to_all | solution.py:142
  861.5 0.6 gather_fusion.4
  862.1 0.6 gather.27
  863.0 0.6 pad_maximum_fusion.7
  (66 shorter events, 2.2 us)
Async XLA Ops:
  6.5 90.3 %all-gather.4.cloned.1.call-start = ((), (), s32[]{:S(2)}) async-start(), calls=%async_computation.3 | async-start | bytes 1892352 | tf_op jit(solution)/shard_map/all_gather | solution.py:72
  7.3 139.1 %all-gather.6.cloned.1.call-start = ((), (), s32[]{:S(2)}) async-start(), calls=%async_computation.4 | async-start | bytes 2228224 | tf_op jit(solution)/shard_map/all_gather | solution.py:42
  7.9 92.7 %copy-start = (bf16[14,256,256]{2,1,0:T(8,128)(2,1)S(1)}, bf16[14,256,256]{2,1,0:T(8,128)(2,1)}, u32[]{:S(2)}) copy-start(bf16[14,256,256]{2,1,0:T(8,128)(2,1)} %param.6) | copy-start | bytes 5505028
  101.1 1.1 copy-start.1
  101.1 3.3 copy-start.10
  101.1 3.4 copy-start.11
  102.1 0.8 copy-start.2
  104.3 205.9 %all-reduce.4.cloned.1.call-start = ((), (), s32[]{:S(2)}) async-start(), calls=%async_computation.5 | async-start | bytes 1048576 | tf_op jit(solution)/shard_map/psum | solution.py:36
  154.6 200.0 %all-gather.8.cloned.1.call-start = ((), (), s32[]{:S(2)}) async-start(), calls=%async_computation.6 | async-start | bytes 2228224 | tf_op jit(solution)/shard_map/all_gather | solution.py:42
  313.1 209.2 %all-reduce.6.cloned.1.call-start = ((), (), s32[]{:S(2)}) async-start(), calls=%async_computation.7 | async-start | bytes 524288 | tf_op jit(solution)/shard_map/psum | solution.py:36
  369.8 230.9 %reduce-scatter.3.cloned.1.call-start = ((), (), s32[]{:S(2)}) async-start(), calls=%async_computation.8 | async-start | bytes 2228224 | tf_op jit(solution)/shard_map/reduce_scatter | solution.py:56
  522.3 3.1 copy-start.3
  523.7 0.7 copy-start.7
  524.7 0.7 copy-start.4
  539.6 220.2 %all-reduce.8.cloned.1.call-start = ((), (), s32[]{:S(2)}) async-start(), calls=%async_computation.9 | async-start | bytes 1048576 | tf_op jit(solution)/shard_map/psum | solution.py:131
  541.3 218.4 %copy-start.5 = (bf16[2,256,256]{2,1,0:T(8,128)(2,1)S(1)}, bf16[2,256,256]{2,1,0:T(8,128)(2,1)}, u32[]{:S(2)}) copy-start(bf16[2,256,256]{2,1,0:T(8,128)(2,1)} %copy-done.4) | copy-start | bytes 786436
  602.8 235.0 %reduce-scatter.5.cloned.1.call-start = ((), (), s32[]{:S(2)}) async-start(), calls=%async_computation.10 | async-start | bytes 2228224 | tf_op jit(solution)/shard_map/reduce_scatter | solution.py:56
  764.6 1.9 copy-start.6
  776.7 61.2 %copy-start.9 = (bf16[1,256,256]{2,1,0:T(8,128)(2,1)S(1)}, bf16[1,256,256]{2,1,0:T(8,128)(2,1)}, u32[]{:S(2)}) copy-start(bf16[1,256,256]{2,1,0:T(8,128)(2,1)} %broadcast_select_fusion.2) | copy-start | bytes 393220
  776.7 75.1 %copy-start.8 = (bf16[4,256,256]{2,1,0:T(8,128)(2,1)S(1)}, bf16[4,256,256]{2,1,0:T(8,128)(2,1)}, u32[]{:S(2)}) copy-start(bf16[4,256,256]{2,1,0:T(8,128)(2,1)} %all-reduce.8.cloned.1.call-done) | copy-start | bytes 1572868
  841.9 19.4 %all-to-all-start = ((bf16[32,2,1024]{2,1,0:T(2,128)(2,1)}), bf16[32,2,1024]{2,1,0:T(2,128)(2,1)S(1)}, u32[]{:S(2)}, u32[]{:S(2)}) async-start(bf16[32,2,1024]{2,1,0:T(2,128)(2,1)} %reshape.589), calls=%async_computation.2 | async-start | bytes 262144 | tf_op jit(solution)/shard_map/all_to_all | solution.py:142
Sparse Core Ops, SparseCore 0:
  10.5 86.2 all-gather.3
  104.5 41.8 all-gather.5
  154.8 155.4 all-reduce.3
  313.2 41.4 all-gather.7
  369.9 152.3 all-reduce.5
  539.7 60.9 reduce-scatter.2
  604.5 155.2 all-reduce.7
  776.8 61.0 reduce-scatter.4
where the time goes:
time: 872 us; the launch traced here: 871 us
  waiting for transfers between devices  759 us (87%)
  local copies, waits for them, and re-layouts  46.5 us (5%)
  matrix products  22.5 us (3%)
  other arithmetic  18.2 us (2%)
  between operations  13.9 us (2%)
  starting transfers between devices  10.3 us (1%)
    psum x2, waiting for transfers between devices, forward_level(): lax.psum(partial_sum.astype(jnp.bfloat16), 'col').astype(jnp.float32)  300 us
    psum x1, waiting for transfers between devices, on_device(): x_mid = lax.psum(spread, 'col').astype(jnp.float32).astype(jnp.bfloat16)  157 us
    reduce_scatter x2, waiting for transfers between devices, scatter_carry(): lax.psum_scatter(jnp.einsum('sq,sbn->qbn', onehot, terms).astype(jnp.bflo...  121 us
    all_gather x1, waiting for transfers between devices, on_device(): whole = lax.all_gather(rhs, 'col', axis=1, tiled=True)  88.9 us
    all_gather x2, waiting for transfers between devices, send_panels(): return lax.all_gather(jnp.stack(pieces), 'row', axis=0, tiled=True)  83.1 us
  transfers between devices with their start and end apart: 9, of which 9 were waited for; matrix products, arithmetic and copies ran while one was open for 1% of the time, Pallas kernels for 0%

commit v1 on v0

--- a/solution.py
+++ b/solution.py
@@ -33,7 +33,9 @@
         jnp.float32
     )
     partial_sum = jnp.einsum("sk,san->kan", onehot, product)
-    summed = lax.psum(partial_sum.astype(jnp.bfloat16), "col").astype(jnp.float32)
+    summed = jnp.sum(lax.all_gather(partial_sum.astype(jnp.bfloat16), "col"), axis=0).astype(
+        jnp.float32
+    )
     return solve_rows(factor_part, target_part - summed)
 
 

time: 872 us -> 822 us (0.943)
  waiting for transfers between devices: 759 us -> 695 us
  other arithmetic: 18.2 us -> 33.4 us
    psum x2 -> x0, waiting for transfers between devices: 300 us -> none  [forward_level(): lax.psum(partial_sum.astype(jnp.bfloat16), 'col').astype(jnp.float32)]
    all_gather x0 -> x2, waiting for transfers between devices: none -> 235 us  [forward_level(): lax.all_gather(partial_sum.astype(jnp.bfloat16), 'col')]
    reduce_sum x0 -> x2, other arithmetic: none -> 15.1 us  [forward_level(): jnp.sum(lax.all_gather(partial_sum.astype(jnp.bfloat16), 'col'), axis=0)]
where the time goes in v1:
time: 822 us; the launch traced here: 821 us
  waiting for transfers between devices  695 us (85%)
  local copies, waits for them, and re-layouts  46.5 us (6%)
  other arithmetic  33.4 us (4%)
  matrix products  22.6 us (3%)
  between operations  14 us (2%)
  starting transfers between devices  10.3 us (1%)
    all_gather x2, waiting for transfers between devices, forward_level(): lax.all_gather(partial_sum.astype(jnp.bfloat16), 'col')  235 us
    psum x1, waiting for transfers between devices, on_device(): x_mid = lax.psum(spread, 'col').astype(jnp.float32).astype(jnp.bfloat16)  156 us
    reduce_scatter x2, waiting for transfers between devices, scatter_carry(): lax.psum_scatter(jnp.einsum('sq,sbn->qbn', onehot, terms).astype(jnp.bflo...  121 us
    all_gather x1, waiting for transfers between devices, on_device(): whole = lax.all_gather(rhs, 'col', axis=1, tiled=True)  88.9 us
    all_gather x2, waiting for transfers between devices, send_panels(): return lax.all_gather(jnp.stack(pieces), 'row', axis=0, tiled=True)  83.8 us
  transfers between devices with their start and end apart: 9, of which 9 were waited for; matrix products, arithmetic and copies ran while one was open for 1% of the time, Pallas kernels for 0%

profile of v1, /device:TPU:8, one launch (start us, length us, event | category | flops | bytes accessed | tf_op | source)
XLA Modules:
  0.0 821.3 jit_solution(9890327454044958263)
XLA Ops:
  6.5 0.7 all-gather.8.cloned.1.call-update
  7.3 0.6 pad_dynamic-slice_fusion.7
  7.9 88.9 %all-gather.8.cloned.1.call-done = bf16[3584,256]{0,1:T(8,128)(2,1)} async-done(((bf16[3584,8]{0,1:T(8,128)(2,1)}), bf16[3584,256]{0,1:T(8,128)(2,1)}) %all-gather.8.cloned.1.call-update) | async-done | bytes 1835024 | tf_op jit(solution)/shard_map/all_gather | solution.py:74
  96.8 2.3 slice.69
  99.1 1.5 copy.115
  100.6 0.4 convolution_convert_fusion
  101.2 0.9 copy-done.1
  102.1 0.8 copy-done.2
  102.9 1.4 maximum_select_fusion
  104.4 41.9 %all-gather.10.cloned.1.call-done = bf16[16,256,256]{2,1,0:T(8,128)(2,1)} async-done(((bf16[1,256,256]{2,1,0:T(8,128)(2,1)}), bf16[16,256,256]{2,1,0:T(8,128)(2,1)}) %all-gather.10.cloned.1.call-update) | async-done | bytes 2097168 | tf_op jit(solution)/shard_map/all_gather | solution.py:44
  146.3 2.2 gather_fusion
  148.6 2.8 convolution_bitcast_fusion.1
  151.4 1.9 copy.118
  153.2 0.5 convolution_convert_fusion.2
  153.7 0.9 copy.119
  154.7 2.2 slice.70
  156.8 1.6 copy.164
  158.4 138.8 %all-gather.14.cloned.1.call-done = bf16[128,256,256]{2,1,0:T(8,128)(2,1)} async-done(((bf16[4,256,256]{2,1,0:T(8,128)(2,1)}), bf16[128,256,256]{2,1,0:T(8,128)(2,1)}) %all-gather.14.cloned.1.call-update) | async-done | bytes 16777232 | tf_op jit(solution)/shard_map/all_gather | solution.py:36
  297.2 9.6 %reduce_sum.24 = bf16[4,256,256]{2,1,0:T(8,128)(2,1)} reduce(bf16[32,4,256,256]{3,2,1,0:T(8,128)(2,1)} %bitcast.177, bf16[]{:T(256)} %constant.203.clone.1), dimensions={0}, to_apply=%region_0.1 | reduce | flops 8126464 | bytes 17301506 | tf_op jit(solution)/shard_map/reduce_sum | solution.py:36
  306.7 1.4 fusion
  308.2 1.4 maximum_select_fusion.1
  309.9 41.9 %all-gather.12.cloned.1.call-done = bf16[16,256,256]{2,1,0:T(8,128)(2,1)} async-done(((bf16[1,256,256]{2,1,0:T(8,128)(2,1)}), bf16[16,256,256]{2,1,0:T(8,128)(2,1)}) %all-gather.12.cloned.1.call-update) | async-done | bytes 2097168 | tf_op jit(solution)/shard_map/all_gather | solution.py:44
  351.8 4.2 add.342
  356.0 3.1 gather_fusion.1
  359.1 2.8 convolution_bitcast_fusion.3
  361.8 2.6 copy.125
  364.4 1.7 convolution_convert_fusion.5
  366.2 0.7 copy.126
  367.1 0.6 compare_and_fusion
  367.6 1.8 slice.71
  369.5 2.0 copy.163
  371.5 95.8 %all-gather.16.cloned.1.call-done = bf16[64,256,256]{2,1,0:T(8,128)(2,1)} async-done(((bf16[2,256,256]{2,1,0:T(8,128)(2,1)}), bf16[64,256,256]{2,1,0:T(8,128)(2,1)}) %all-gather.16.cloned.1.call-update) | async-done | bytes 8388624 | tf_op jit(solution)/shard_map/all_gather | solution.py:36
  467.3 5.5 reduce_sum.25
  472.8 1.4 convolution_convert_fusion.3
  474.2 0.7 copy-done.7
  475.2 0.7 copy-done.4
  475.9 1.6 pad_maximum_fusion.2
  477.5 3.0 gather_fusion.2
  480.6 2.8 convolution_bitcast_fusion.2
  483.3 2.6 copy.134
  485.9 2.1 fusion.46
  488.0 2.0 copy.160
  490.2 1.7 broadcast_select_fusion.2
  491.8 60.0 %reduce-scatter.3.cloned.1.call-done = bf16[1,256,256]{2,1,0:T(8,128)(2,1)} async-done(((bf16[16,256,256]{2,1,0:T(8,128)(2,1)}), bf16[1,256,256]{2,1,0:T(8,128)(2,1)}) %reduce-scatter.3.cloned.1.call-update) | async-done | bytes 131088 | tf_op jit(solution)/shard_map/reduce_scatter | solution.py:58
  551.9 1.2 convolution_convert_fusion.7
  553.0 0.9 broadcast_select_fusion
  554.3 156.2 %all-reduce.2.cloned.1.call-done = bf16[4,256,256]{2,1,0:T(8,128)(2,1)} async-done(((bf16[4,256,256]{2,1,0:T(8,128)(2,1)}), bf16[4,256,256]{2,1,0:T(8,128)(2,1)}) %all-reduce.2.cloned.1.call-update) | async-done | bytes 524304 | tf_op jit(solution)/shard_map/psum | solution.py:133
  710.5 2.7 pad_maximum_fusion.1
  713.2 2.2 gather_fusion.3
  715.4 1.9 convolution_bitcast_fusion
  717.3 1.4 pad_maximum_fusion
  718.7 4.5 copy.137
  723.2 2.3 fusion.42
  725.4 2.0 copy.159
  727.6 61.1 %reduce-scatter.5.cloned.1.call-done = bf16[1,256,256]{2,1,0:T(8,128)(2,1)} async-done(((bf16[16,256,256]{2,1,0:T(8,128)(2,1)}), bf16[1,256,256]{2,1,0:T(8,128)(2,1)}) %reduce-scatter.5.cloned.1.call-update) | async-done | bytes 131088 | tf_op jit(solution)/shard_map/reduce_scatter | solution.py:58
  788.7 1.1 fusion.3
  790.2 0.5 broadcast.811
  790.7 1.1 reduce.2
  792.0 0.7 reshape.591
  792.7 9.8 %all-to-all-start = ((bf16[32,2,1024]{2,1,0:T(2,128)(2,1)}), bf16[32,2,1024]{2,1,0:T(2,128)(2,1)S(1)}, u32[]{:S(2)}, u32[]{:S(2)}) async-start(bf16[32,2,1024]{2,1,0:T(2,128)(2,1)} %reshape.591), calls=%async_computation.2 | async-start | bytes 262144 | tf_op jit(solution)/shard_map/all_to_all | solution.py:144
  803.0 9.2 %all-to-all-done = bf16[32,2,1024]{2,1,0:T(2,128)(2,1)S(1)} async-done(((bf16[32,2,1024]{2,1,0:T(2,128)(2,1)}), bf16[32,2,1024]{2,1,0:T(2,128)(2,1)S(1)}, u32[]{:S(2)}, u32[]{:S(2)}) %all-to-all-start) | async-done | bytes 131104 | tf_op jit(solution)/shard_map/all_to_all | solution.py:144
  812.3 0.6 gather_fusion.4
  812.9 0.6 gather.27
  813.8 0.6 pad_maximum_fusion.7
  (68 shorter events, 2.9 us)
Async XLA Ops:
  6.5 90.3 %all-gather.8.cloned.1.call-start = ((), (), s32[]{:S(2)}) async-start(), calls=%async_computation.3 | async-start | bytes 1892352 | tf_op jit(solution)/shard_map/all_gather | solution.py:74
  7.3 139.1 %all-gather.10.cloned.1.call-start = ((), (), s32[]{:S(2)}) async-start(), calls=%async_computation.4 | async-start | bytes 2228224 | tf_op jit(solution)/shard_map/all_gather | solution.py:44
  7.9 92.7 %copy-start = (bf16[14,256,256]{2,1,0:T(8,128)(2,1)S(1)}, bf16[14,256,256]{2,1,0:T(8,128)(2,1)}, u32[]{:S(2)}) copy-start(bf16[14,256,256]{2,1,0:T(8,128)(2,1)} %param.6) | copy-start | bytes 5505028
  101.1 1.0 copy-start.1
  101.1 3.2 copy-start.10
  101.1 3.3 copy-start.11
  102.1 0.8 copy-start.2
  104.3 192.9 %all-gather.14.cloned.1.call-start = ((), (), s32[]{:S(2)}) async-start(), calls=%async_computation.9 | async-start | bytes 17301504 | tf_op jit(solution)/shard_map/all_gather | solution.py:36
  154.6 197.2 %all-gather.12.cloned.1.call-start = ((), (), s32[]{:S(2)}) async-start(), calls=%async_computation.5 | async-start | bytes 2228224 | tf_op jit(solution)/shard_map/all_gather | solution.py:44
  309.6 157.7 %all-gather.16.cloned.1.call-start = ((), (), s32[]{:S(2)}) async-start(), calls=%async_computation.10 | async-start | bytes 8650752 | tf_op jit(solution)/shard_map/all_gather | solution.py:36
  366.9 184.9 %reduce-scatter.3.cloned.1.call-start = ((), (), s32[]{:S(2)}) async-start(), calls=%async_computation.6 | async-start | bytes 2228224 | tf_op jit(solution)/shard_map/reduce_scatter | solution.py:58
  472.8 3.1 copy-start.3
  474.2 0.7 copy-start.7
  475.2 0.7 copy-start.4
  490.1 220.4 %all-reduce.2.cloned.1.call-start = ((), (), s32[]{:S(2)}) async-start(), calls=%async_computation.7 | async-start | bytes 1048576 | tf_op jit(solution)/shard_map/psum | solution.py:133
  554.0 234.7 %reduce-scatter.5.cloned.1.call-start = ((), (), s32[]{:S(2)}) async-start(), calls=%async_computation.8 | async-start | bytes 2228224 | tf_op jit(solution)/shard_map/reduce_scatter | solution.py:58
  715.4 1.9 copy-start.6
  727.5 61.2 %copy-start.9 = (bf16[1,256,256]{2,1,0:T(8,128)(2,1)S(1)}, bf16[1,256,256]{2,1,0:T(8,128)(2,1)}, u32[]{:S(2)}) copy-start(bf16[1,256,256]{2,1,0:T(8,128)(2,1)} %broadcast_select_fusion.2) | copy-start | bytes 393220
  727.5 75.1 %copy-start.5 = (bf16[2,256,256]{2,1,0:T(8,128)(2,1)S(1)}, bf16[2,256,256]{2,1,0:T(8,128)(2,1)}, u32[]{:S(2)}) copy-start(bf16[2,256,256]{2,1,0:T(8,128)(2,1)} %copy-done.4) | copy-start | bytes 786436
  727.5 75.1 %copy-start.8 = (bf16[4,256,256]{2,1,0:T(8,128)(2,1)S(1)}, bf16[4,256,256]{2,1,0:T(8,128)(2,1)}, u32[]{:S(2)}) copy-start(bf16[4,256,256]{2,1,0:T(8,128)(2,1)} %all-reduce.2.cloned.1.call-done) | copy-start | bytes 1572868
  792.7 19.4 %all-to-all-start = ((bf16[32,2,1024]{2,1,0:T(2,128)(2,1)}), bf16[32,2,1024]{2,1,0:T(2,128)(2,1)S(1)}, u32[]{:S(2)}, u32[]{:S(2)}) async-start(bf16[32,2,1024]{2,1,0:T(2,128)(2,1)} %reshape.591), calls=%async_computation.2 | async-start | bytes 262144 | tf_op jit(solution)/shard_map/all_to_all | solution.py:144
Sparse Core Ops, SparseCore 0:
  10.5 86.2 all-gather.7
  104.4 41.8 all-gather.9
  154.7 142.3 all-gather.13
  309.7 42.0 all-gather.11
  367.0 100.1 all-gather.15
  490.2 61.6 reduce-scatter.2
  555.2 155.2 all-reduce.1
  727.6 61.0 reduce-scatter.4
